TPU v7x, 32 devices: a whole 2x2x4 slice. The times are simulated.
32 devices in a mesh: atoms: 16 (over z, x, core), waves: 2 (over y).
Axes of the slice: x: 2, y: 2, z: 4, core: 2. Of those that a mesh axis runs over, the one named last changes fastest.
Arguments:
- features: bfloat16 [64, 32768], P(None, 'atoms'), may hold values from -6 to 6
- coords: float32 [3, 32768], P(None, 'atoms'), may hold values from 0 to 1
- neighbours: int32 [27, 256], P(None, 'atoms'), may hold values from 0 to 255, as said below
- live_slots: int32 [27, 256], P(None, 'atoms'), may hold values 0 or 1
- block_count: int32 [16], P('atoms'), may hold values from 8 to 16, as said below
- kvec: int32 [3, 4096], P(None, 'waves'), may hold values from -32 to 32, as said below
- msg_weight: bfloat16 [1, 64, 64], replicated, may hold values from -0.75 to 0.75
- filter_weight: float32 [1, 64, 64], replicated, may hold values from -0.75 to 0.75
- mlp_in: bfloat16 [1, 128, 192], replicated, may hold values from -0.4375 to 0.4375
- mlp_out: bfloat16 [1, 64, 128], replicated, may hold values from -0.5 to 0.5
Outputs:
- updated: bfloat16 [64, 32768], P(None, 'atoms')
Inputs may be any that keep to these rules, and one draw needn't show every extreme that they name: `neighbours`: entry [s, b] names a block slot whose index of atoms, slot // 16, equals b // 16 or lies one before or one after it, cyclically, and which is live. `block_count`: some index of atoms has all 16 of its slots live in every draw. `kvec`: rows 1 and 2 lie in -5 to 5; no column is zero in all three rows.
All inputs are finite; a program needn't handle non-finite values. No bound on the sum of `live_slots` on one device may be relied on, other than what follows from the above.
Results may differ from a plain program's by a relative error of at most 0.0062.
Values may be sent and summed in bfloat16 or wider, within the bound.
A program may use at most 64 MiB of HBM per device.

v0:
```python
import functools
import math

import jax
import jax.numpy as jnp
from jax import lax
from jax.experimental import pallas as pl
from jax.experimental.pallas import tpu as pltpu
from jax.sharding import PartitionSpec as P

BLOCK = 128
MSG_SCALE = 0.125
GAIN_TOP = 20.0
SIDE = 5
BASE = 2 * SIDE + 1
HALF = (BASE * BASE + 1) // 2
BATCH = 4
F32 = jnp.float32
BF16 = jnp.bfloat16
VMEM = pl.BlockSpec(memory_space=pltpu.VMEM)
SMEM = pl.BlockSpec(memory_space=pltpu.SMEM)
NT = (((1,), (1,)), ((), ()))
TN = (((0,), (0,)), ((), ()))
PARAMS = pltpu.CompilerParams(vmem_limit_bytes=48 * 1024 * 1024)


def phase_rows(ta, tb_ref, pair, held):
    half = tb_ref.shape[0] // 2
    cb = tb_ref[pl.ds(pair, 1), :].astype(BF16)
    sb = tb_ref[pl.ds(half + pair, 1), :].astype(BF16)
    return ta * cb, ta * sb


def groups_of(count):
    return [(i, min(4, count - i)) for i in range(0, count, 4)]


def structure_kernel(pairs, ta_ref, tb_ref, h_ref, out_ref):
    a = ta_ref.shape[0]
    out_ref[...] = jnp.zeros_like(out_ref)
    ta = ta_ref[...]
    h = h_ref[...]
    for first, size in groups_of(pairs):
        cs, ss = zip(*[phase_rows(ta, tb_ref, first + i, pairs) for i in range(size)])
        rows = slice(first * a, (first + size) * a)
        out_ref[rows, 0:64] = lax.dot_general(jnp.concatenate(cs, 0), h, NT, preferred_element_type=F32)
        out_ref[rows, 64:128] = lax.dot_general(jnp.concatenate(ss, 0), h, NT, preferred_element_type=F32)
    rows = tb_ref.shape[0]
    out_ref[pairs * a : pairs * a + rows, 0:64] = lax.dot_general(
        tb_ref[...].astype(BF16), h, NT, preferred_element_type=F32
    )


def potentials_kernel(pairs, scale, ta_ref, tb_ref, g_ref, out_ref):
    a = ta_ref.shape[0]
    ta = ta_ref[...]
    rows = tb_ref.shape[0]
    acc = lax.dot_general(
        g_ref[pairs * a : pairs * a + rows, 0:64], tb_ref[...].astype(BF16), TN, preferred_element_type=F32
    )
    for first, size in groups_of(pairs):
        cs, ss = zip(*[phase_rows(ta, tb_ref, first + i, pairs) for i in range(size)])
        g = g_ref[first * a : (first + size) * a, :]
        acc += lax.dot_general(g[:, 0:64], jnp.concatenate(cs, 0), TN, preferred_element_type=F32)
        acc += lax.dot_general(g[:, 64:128], jnp.concatenate(ss, 0), TN, preferred_element_type=F32)
    out_ref[...] = (acc * scale).astype(BF16)


def short_kernel(scale_x, idx_ref, live_ref, own_ref, near_ref, hm_ref, out_ref):
    blocks = own_ref.shape[0]
    steps = idx_ref.shape[0] // BATCH

    def block_step(b, _):
        own = own_ref[b]
        cols = [jnp.broadcast_to(own[:, d : d + 1], (BLOCK, BLOCK)) for d in range(3)]

        def slot_step(step, acc):
            weights, mapped = [], []
            for u in range(BATCH):
                s = step * BATCH + u
                n = idx_ref[s, b]
                near = near_ref[n]
                total = None
                for d in (1, 2, 0):
                    diff = cols[d] - near[d : d + 1, :]
                    diff = diff - jnp.round(diff)
                    if d == 0:
                        diff = diff * scale_x
                    total = diff * diff if total is None else total + diff * diff
                weights.append(jnp.exp(-2.0 * total).astype(BF16))
                mapped.append(hm_ref[n] * live_ref[s, b].astype(BF16))
            return acc + lax.dot_general(
                jnp.concatenate(mapped, 1), jnp.concatenate(weights, 1), NT, preferred_element_type=F32
            )

        acc = lax.fori_loop(0, steps, slot_step, jnp.zeros((hm_ref.shape[1], BLOCK), F32))
        out_ref[b] = (acc * MSG_SCALE).astype(BF16)
        return 0

    lax.fori_loop(0, blocks, block_step, 0)


def update_kernel(count_ref, h_ref, msg_ref, pot_ref, first_ref, second_ref, out_ref):
    h = h_ref[...]
    pot = pot_ref[0].astype(F32)
    for w in range(1, pot_ref.shape[0]):
        pot = pot + pot_ref[w].astype(F32)
    msg = jnp.concatenate([msg_ref[b] for b in range(msg_ref.shape[0])], 1)
    z = jnp.concatenate([h, msg, pot.astype(BF16)], 0)
    hidden = jnp.dot(first_ref[...], z, preferred_element_type=F32)
    hidden = (hidden * jax.nn.sigmoid(hidden)).astype(BF16)
    out = h.astype(F32) + jnp.dot(second_ref[...], hidden, preferred_element_type=F32)
    atom = lax.broadcasted_iota(jnp.int32, out.shape, 1)
    out_ref[...] = jnp.where(atom < count_ref[0] * BLOCK, out, 0.0).astype(BF16)


def call(kernel, shape, dtype, specs, *args):
    return pl.pallas_call(
        kernel,
        out_shape=jax.ShapeDtypeStruct(shape, dtype),
        in_specs=specs,
        out_specs=VMEM,
        compiler_params=PARAMS,
    )(*args)


def coefficients(kvec, regions, pairs, padded, first):
    top = 2 * regions
    k = jnp.where(kvec[0:1] < 0, -kvec, kvec)
    code = k[1] * BASE + k[2]
    n = jnp.abs(code) - first
    onehot_a = (jnp.arange(top + 1, dtype=F32)[:, None] == k[0][None, :]).astype(BF16)
    which = jnp.arange(pairs, dtype=F32)[:, None] == n[None, :]
    up = (which & (code >= 0)[None, :]).astype(BF16)
    down = (which & (code < 0)[None, :]).astype(BF16)
    m1 = lax.dot_general(up, onehot_a, NT, preferred_element_type=F32)
    m2 = lax.dot_general(down, onehot_a, NT, preferred_element_type=F32)
    b = jnp.arange(pairs, dtype=F32) + first
    ky = jnp.floor((b + SIDE) / BASE)
    kz = b - ky * BASE
    kx = jnp.arange(top + 1, dtype=F32) / regions
    gain = GAIN_TOP / (4.0 + (kx * kx)[None, :] + (ky * ky + kz * kz)[:, None])
    p = gain * (m1 + m2)
    q = gain * (m2 - m1)
    main_p, main_q = p[:, 1:], q[:, 1:]
    a = 2 * top
    p_rows = jnp.concatenate([main_p, main_p], 1).reshape(-1)
    q_cos = jnp.concatenate([main_q, -main_q], 1).reshape(-1)
    extra = jnp.pad(p[:, 0], (0, a // 2 - pairs))
    extra = jnp.concatenate([extra, extra])
    rest = (padded - pairs - 1) * a
    p_cos = jnp.concatenate([p_rows, extra, jnp.zeros((rest,), F32)])
    p_sin = jnp.concatenate([p_rows, jnp.zeros((a + rest,), F32)])
    q_cos = jnp.pad(q_cos, (0, a + rest))
    return jnp.stack([p_cos, p_sin, q_cos])


def local(
    features,
    coords,
    neighbours,
    live_slots,
    block_count,
    kvec,
    msg_weight,
    filter_weight,
    mlp_in,
    mlp_out,
):
    chans, width = features.shape
    nblocks = width // BLOCK
    regions = lax.axis_size("atoms")
    groups = lax.axis_size("waves")
    here = lax.axis_index("atoms")
    wave = lax.axis_index("waves")
    total = regions * width
    waves_total = kvec.shape[1] * groups
    top = 2 * regions
    a = 2 * top
    pairs = -(-HALF // groups)
    padded = -(-(pairs + 1) // regions) * regions
    first = (wave * pairs).astype(F32)

    h = features
    live = jnp.arange(width, dtype=jnp.int32) < block_count[0] * BLOCK
    masked = jnp.where(live[None, :], h, jnp.zeros_like(h))

    forward = [(i, (i + 1) % regions) for i in range(regions)]
    backward = [((i + 1) % regions, i) for i in range(regions)]
    hm = jnp.dot(msg_weight[0], h, preferred_element_type=F32).astype(BF16)
    hm3 = hm.reshape(chans, nblocks, BLOCK).transpose(1, 0, 2)
    pos3 = coords.reshape(3, nblocks, BLOCK).transpose(1, 0, 2)
    near = jnp.concatenate([lax.ppermute(pos3, "atoms", forward), pos3, lax.ppermute(pos3, "atoms", backward)], 0)
    hm_ext = jnp.concatenate([lax.ppermute(hm3, "atoms", forward), hm3, lax.ppermute(hm3, "atoms", backward)], 0)

    def turns(t, quarter):
        t = t - jnp.round(t)
        return jnp.cos((2.0 * math.pi) * (t - quarter))

    quarter = jnp.array([0.0, 0.25], F32)[:, None, None]
    ka = jnp.arange(1, top + 1, dtype=F32)
    ta = turns((ka[:, None] * coords[0][None, :])[None], quarter).reshape(a, width).astype(BF16)
    b = jnp.arange(top, dtype=F32) + first
    ky = jnp.floor((b + SIDE) / BASE)
    kz = b - ky * BASE
    tb = turns((ky[:, None] * coords[1][None, :] + kz[:, None] * coords[2][None, :])[None], quarter)
    tb = tb.reshape(a, width)

    factor = call(
        functools.partial(structure_kernel, pairs), (padded * a, 2 * chans), F32, [VMEM] * 3, ta, tb, masked
    )
    share = lax.psum_scatter(factor, "atoms", scatter_dimension=0, tiled=True)

    source = neighbours // nblocks
    offset = (source - here) % regions
    which = jnp.where(offset == 0, 1, jnp.where(offset == 1, 2, 0))
    ext_index = which * nblocks + neighbours % nblocks
    mine = nblocks // groups
    slots = neighbours.shape[0]
    extra = -slots % BATCH
    start = wave * mine
    idx = jnp.pad(lax.dynamic_slice_in_dim(ext_index, start, mine, 1), ((0, extra), (0, 0)))
    used = jnp.pad(lax.dynamic_slice_in_dim(live_slots, start, mine, 1), ((0, extra), (0, 0))).astype(F32)
    own = lax.dynamic_slice_in_dim(pos3, start, mine, 0).transpose(0, 2, 1)
    msg = call(
        functools.partial(short_kernel, float(regions)),
        (mine, chans, BLOCK),
        BF16,
        [SMEM, SMEM, VMEM, VMEM, VMEM],
        idx,
        used,
        own,
        near,
        hm_ext,
    )
    msg = lax.all_gather(msg, "waves", axis=0, tiled=True)

    all_k = lax.all_gather(kvec.astype(F32), "waves", axis=1, tiled=True)
    coef = coefficients(all_k, regions, pairs, padded, first)
    owned = padded * a // regions
    coef = lax.dynamic_slice_in_dim(coef, here * owned, owned, 1)
    scaled = share * (1.0 / math.sqrt(total))
    mixing = filter_weight[0]
    cos_part = jnp.dot(scaled[:, :chans], mixing, precision=lax.Precision.HIGHEST)
    sin_part = jnp.dot(scaled[:, chans:], mixing, precision=lax.Precision.HIGHEST)

    def partner(x):
        y = x.reshape(-1, 2, a // 2, chans)
        return jnp.concatenate([y[:, 1:], y[:, :1]], 1).reshape(-1, chans)

    g_cos = coef[0][:, None] * cos_part + coef[2][:, None] * partner(sin_part)
    g_sin = coef[1][:, None] * sin_part - coef[2][:, None] * partner(cos_part)
    filtered = lax.all_gather(jnp.concatenate([g_cos, g_sin], 1).astype(BF16), "atoms", axis=0, tiled=True)

    part = call(
        functools.partial(potentials_kernel, pairs, 1.0 / math.sqrt(waves_total)),
        (chans, width),
        BF16,
        [VMEM] * 3,
        ta,
        tb,
        filtered,
    )
    parts = lax.all_gather(part, "waves", axis=0)
    return call(
        update_kernel,
        (chans, width),
        BF16,
        [SMEM] + [VMEM] * 5,
        block_count,
        h,
        msg,
        parts,
        mlp_in[0],
        mlp_out[0],
    )


def solution(mesh):
    in_specs = (
        P(None, "atoms"),
        P(None, "atoms"),
        P(None, "atoms"),
        P(None, "atoms"),
        P("atoms"),
        P(None, "waves"),
        P(),
        P(),
        P(),
        P(),
    )
    out_specs = P(None, "atoms")
    return jax.shard_map(local, mesh=mesh, in_specs=in_specs, out_specs=out_specs, check_vma=False)
```

profile of v0, /device:TPU:0, one launch (start us, length us, event | category | flops | bytes accessed | tf_op | source)
XLA Modules:
  0.0 130.4 jit_solution(6224397101184698457)
XLA Ops:
  6.5 0.0 copy-start
  6.5 0.0 reduce-scatter.2.cloned.1.call-start
  6.5 5.4 %collective-permute-start.1 = (f32[16,3,128]{2,1,0:T(4,128)}, f32[16,3,128]{2,1,0:T(4,128)S(1)}, u32[]{:S(2)}, u32[]{:S(2)}) collective-permute-start(f32[16,3,128]{2,1,0:T(4,128)} %bitcast.76), channel_id=1, source_target_pairs={{2,0},{4,2},{6,4},{8,6},{10,8},{12,10},{14,12},{16,14},{18,16},{20... | collective-permute-start | bytes 73736 | tf_op jit(solution)/shard_map/ppermute | solution.py:193
  12.0 0.0 collective-permute-start
  12.0 1.2 fusion
  13.1 0.0 copy-start.3
  13.2 0.0 copy-start.1
  13.2 0.1 copy.54
  13.2 4.5 %collective-permute-start.3 = (bf16[16,64,128]{2,1,0:T(8,128)(2,1)S(1)}, bf16[16,64,128]{2,1,0:T(8,128)(2,1)S(1)}, u32[]{:S(2)}, u32[]{:S(2)}) collective-permute-start(bf16[16,64,128]{2,1,0:T(8,128)(2,1)S(1)} %bitcast.71), channel_id=1, source_target_pairs={{2,0},{4,2},{6,4},{8,6},{10,8},{12,10},{14,12},{16,14},{18,16},{20... | collective-permute-start | bytes 786440 | tf_op jit(solution)/shard_map/ppermute | solution.py:194
  17.7 0.0 collective-permute-start.2
  17.7 0.0 copy-done.3
  18.4 0.0 copy-start.8
  18.4 0.6 copy-done.8
  19.1 0.1 sub.95
  19.1 0.1 sub.96
  19.2 0.0 copy-done.1
  19.3 0.1 round-nearest-even_subtract_fusion.1
  19.4 0.1 round-nearest-even_subtract_fusion
  19.5 3.4 %fusion.4 = (f32[64,2048]{1,0:T(8,128)S(1)}, bf16[64,2048]{1,0:T(8,128)(2,1)S(1)}) fusion(f32[32,2048]{1,0:T(8,128)S(1)} %round-nearest-even_subtract_fusion, f32[64]{0:T(128)S(1)} %sub.96, f32[32,2048]{1,0:T(8,128)S(1)} %round-nearest-even_subtract_fusion.1), kind=kLoop, calls=%fused_computation.8 | loop fusion | flops 655360 | bytes 1310976 | tf_op jit(solution)/shard_map/cos | solution.py:198
  22.9 5.5 %shard_map.110 = f32[2048,128]{1,0:T(8,128)} custom-call(bf16[64,2048]{1,0:T(8,128)(2,1)S(1)} %get-tuple-element.28.ta_ref, f32[64,2048]{1,0:T(8,128)S(1)} %get-tuple-element.27.tb_ref, bf16[64,2048]{1,0:T(8,128)(2,1)S(1)} %broadcast_select_fusion.h_ref), custom_call_target="tpu_custom_call" | custom-call | tf_op jit(solution)/shard_map/pallas_call | solution.py:118
  28.5 0.0 reduce-scatter.2.cloned.1.call-update
  28.5 0.7 copy-done.5
  29.2 4.6 %all_gather.16 = f32[3,4096]{1,0:T(4,128)S(1)} all-gather(f32[3,2048]{1,0:T(4,128)S(1)} %convert_element_type.27), channel_id=1, replica_groups=mesh['atoms'=16,'waves'=2] {'waves'}, dimensions={1}, use_global_device_ids=true | all-gather | bytes 73728 | tf_op jit(solution)/shard_map/all_gather | solution.py:238
  33.8 0.1 compare_reduce_fusion.2
  33.9 0.1 compare_reduce_fusion
  34.1 0.3 fusion.1
  34.4 0.3 add_multiply_fusion
  34.7 0.1 slice.90
  34.8 0.1 pad_maximum_fusion.5
  34.9 0.1 fusion.35
  34.9 0.1 pad_maximum_fusion.6
  35.0 0.6 copy-done.7
  35.7 0.7 copy-done.6
  36.4 0.1 copy.37
  36.4 0.1 copy.51
  36.5 0.1 reshape.173
  36.6 0.1 reshape.172
  36.7 0.1 slice_reduce_fusion
  36.8 0.1 concatenate.31
  36.9 0.1 fusion.34
  37.1 0.1 fusion.30
  37.2 0.0 copy-start.4
  37.2 0.2 copy.43.own_ref
  37.4 0.6 copy-done.4
  38.0 0.1 copy.48
  38.1 0.0 collective-permute-done.1
  38.1 0.0 collective-permute-done
  38.1 0.0 collective-permute-done.3
  38.1 0.0 collective-permute-done.2
  38.2 0.1 pad_maximum_fusion.hm_ref
  38.3 19.5 %shard_map.109 = bf16[8,64,128]{2,1,0:T(8,128)(2,1)S(1)} custom-call(s32[28,8]{1,0:T(8,128)S(1)} %pad.16.idx_ref, f32[28,8]{1,0:T(8,128)S(1)} %pad_convert_fusion.live_ref, f32[8,128,3]{2,1,0:T(8,128)S(1)} %copy.43.own_ref, f32[48,3,128]{2,1,0:T(4,128)S(1)} %pad_maximum_fusion.1.near_ref, bf16[48,64,128]{2,1,0:T(8,128)(2,1)S(1)} %pad_maximum_fusion.hm_ref), custom_call_target="tpu_custom_call" | custom-call | tf_op jit(solution)/shard_map/pallas_call | solution.py:118
  57.7 5.6 %all_gather.15.msg_ref = bf16[16,64,128]{2,1,0:T(8,128)(2,1)S(1)} all-gather(bf16[8,64,128]{2,1,0:T(8,128)(2,1)S(1)} %shard_map.109), channel_id=1, replica_groups=mesh['atoms'=16,'waves'=2] {'waves'}, dimensions={0}, use_global_device_ids=true | all-gather | bytes 393216 | tf_op jit(solution)/shard_map/all_gather | solution.py:236
  63.4 24.1 %reduce-scatter.2.cloned.1.call-done = f32[128,128]{1,0:T(8,128)} async-done(((f32[2048,128]{1,0:T(8,128)}), f32[128,128]{1,0:T(8,128)}) %reduce-scatter.2.cloned.1.call-update) | async-done | bytes 65552 | tf_op jit(solution)/shard_map/reduce_scatter | solution.py:212
  87.4 0.8 broadcast_multiply_fusion
  88.3 0.3 fusion.18
  88.6 0.2 fusion.20
  88.8 0.1 fusion.25
  88.9 0.1 pad_maximum_fusion.4
  89.0 21.0 %all_gather.17.g_ref = bf16[2048,128]{1,0:T(8,128)(2,1)S(1)} all-gather(bf16[128,128]{1,0:T(8,128)(2,1)S(1)} %pad_maximum_fusion.4), channel_id=1, replica_groups=mesh['atoms'=16,'waves'=2] {'atoms'}, dimensions={0}, use_global_device_ids=true | all-gather | bytes 557056 | tf_op jit(solution)/shard_map/all_gather | solution.py:253
  110.0 3.1 %shard_map.111 = bf16[64,2048]{1,0:T(8,128)(2,1)S(1)} custom-call(bf16[64,2048]{1,0:T(8,128)(2,1)S(1)} %get-tuple-element.28.ta_ref, f32[64,2048]{1,0:T(8,128)S(1)} %get-tuple-element.27.tb_ref, bf16[2048,128]{1,0:T(8,128)(2,1)S(1)} %all_gather.17.g_ref), custom_call_target="tpu_custom_call" | custom-call | tf_op jit(solution)/shard_map/pallas_call | solution.py:118
  113.1 0.0 copy-start.2
  113.1 9.2 %all-gather = bf16[128,2048]{1,0:T(8,128)(2,1)S(1)} all-gather(bf16[64,2048]{1,0:T(8,128)(2,1)S(1)} %shard_map.111), channel_id=2, replica_groups=mesh['atoms'=16,'waves'=2] {'waves'}, dimensions={0}, use_global_device_ids=true | all-gather | bytes 786432 | tf_op jit(solution)/shard_map/all_gather | solution.py:264
  122.3 0.0 copy-done.2
  122.4 1.2 shard_map.112
  (30 shorter events, 0.3 us)
Async XLA Ops:
  6.5 81.8 %copy-start = (f32[1,64,64]{2,1,0:T(8,128)S(1)}, f32[1,64,64]{2,1,0:T(8,128)}, u32[]{:S(2)}) copy-start(f32[1,64,64]{2,1,0:T(8,128)} %param.18) | copy-start | bytes 49156
  6.5 80.9 %reduce-scatter.2.cloned.1.call-start = ((), (), s32[]{:S(2)}) async-start(), calls=%async_computation.1 | async-start | bytes 1114112 | tf_op jit(solution)/shard_map/reduce_scatter | solution.py:212
  6.5 31.5 %collective-permute-start.1 = (f32[16,3,128]{2,1,0:T(4,128)}, f32[16,3,128]{2,1,0:T(4,128)S(1)}, u32[]{:S(2)}, u32[]{:S(2)}) collective-permute-start(f32[16,3,128]{2,1,0:T(4,128)} %bitcast.76), channel_id=1, source_target_pairs={{2,0},{4,2},{6,4},{8,6},{10,8},{12,10},{14,12},{16,14},{18,16},{20... | collective-permute-start | bytes 73736 | tf_op jit(solution)/shard_map/ppermute | solution.py:193
  12.0 26.1 %collective-permute-start = (f32[16,3,128]{2,1,0:T(4,128)}, f32[16,3,128]{2,1,0:T(4,128)S(1)}, u32[]{:S(2)}, u32[]{:S(2)}) collective-permute-start(f32[16,3,128]{2,1,0:T(4,128)} %bitcast.77), channel_id=1, source_target_pairs={{0,2},{2,4},{4,6},{6,8},{8,10},{10,12},{12,14},{14,16},{16,18},{18... | collective-permute-start | bytes 73736 | tf_op jit(solution)/shard_map/ppermute | solution.py:193
  13.1 4.6 %copy-start.3 = (f32[3,2048]{1,0:T(4,128)S(1)}, f32[3,2048]{1,0:T(4,128)}, u32[]{:S(2)}) copy-start(f32[3,2048]{1,0:T(4,128)} %param.12) | copy-start | bytes 73732
  13.2 6.1 %copy-start.1 = (bf16[64,2048]{1,0:T(8,128)(2,1)S(1)}, bf16[64,2048]{1,0:T(8,128)(2,1)}, u32[]{:S(2)}) copy-start(bf16[64,2048]{1,0:T(8,128)(2,1)} %h_ref.1) | copy-start | bytes 786436
  13.2 24.9 %collective-permute-start.3 = (bf16[16,64,128]{2,1,0:T(8,128)(2,1)S(1)}, bf16[16,64,128]{2,1,0:T(8,128)(2,1)S(1)}, u32[]{:S(2)}, u32[]{:S(2)}) collective-permute-start(bf16[16,64,128]{2,1,0:T(8,128)(2,1)S(1)} %bitcast.71), channel_id=1, source_target_pairs={{2,0},{4,2},{6,4},{8,6},{10,8},{12,10},{14,12},{16,14},{18,16},{20... | collective-permute-start | bytes 786440 | tf_op jit(solution)/shard_map/ppermute | solution.py:194
  17.7 20.4 %collective-permute-start.2 = (bf16[16,64,128]{2,1,0:T(8,128)(2,1)S(1)}, bf16[16,64,128]{2,1,0:T(8,128)(2,1)S(1)}, u32[]{:S(2)}, u32[]{:S(2)}) collective-permute-start(bf16[16,64,128]{2,1,0:T(8,128)(2,1)S(1)} %bitcast.72), channel_id=1, source_target_pairs={{0,2},{2,4},{4,6},{6,8},{8,10},{10,12},{12,14},{14,16},{16,18},{18... | collective-permute-start | bytes 786440 | tf_op jit(solution)/shard_map/ppermute | solution.py:194
  18.4 0.7 copy-start.8
  28.4 0.8 copy-start.5
  34.9 0.7 copy-start.7
  35.7 0.7 copy-start.6
  37.2 0.8 copy-start.4
  113.1 9.3 %copy-start.2 = (bf16[1,64,128]{2,1,0:T(8,128)(2,1)S(1)}, bf16[1,64,128]{2,1,0:T(8,128)(2,1)}, u32[]{:S(2)}) copy-start(bf16[1,64,128]{2,1,0:T(8,128)(2,1)} %param.20) | copy-start | bytes 49156
Sparse Core Ops, SparseCore 0:
  28.6 58.7 reduce-scatter.1
where the time goes:
time: 131 us; the launch traced here: 130 us
  blocking collectives  40.4 us (31%)
  Pallas kernels  29.2 us (22%)
  waiting for transfers between devices  24.1 us (18%)
  between operations  14.4 us (11%)
  starting transfers between devices  9.92 us (8%)
  other arithmetic  5.59 us (4%)
  local copies, waits for them, and re-layouts  4.47 us (3%)
  matrix products  2.24 us (2%)
    pallas_call x4, Pallas kernels, call(): pl.pallas_call(kernel, out_shape=jax.ShapeDtypeStruct(shape, dtype), in_s...  29.2 us
    reduce_scatter x1, waiting for transfers between devices, local(): share = lax.psum_scatter(factor, 'atoms', scatter_dimension=0, tiled=True)  24.1 us
    all_gather x1, blocking collectives, local(): lax.all_gather(jnp.concatenate([g_cos, g_sin], 1).astype(BF16), 'atoms',...  21 us
    all_gather x1, blocking collectives, local(): parts = lax.all_gather(part, 'waves', axis=0)  9.25 us
    all_gather x1, blocking collectives, local(): msg = lax.all_gather(msg, 'waves', axis=0, tiled=True)  5.64 us
    ppermute x1, starting transfers between devices, local(): lax.ppermute(pos3, 'atoms', backward)  5.42 us
    all_gather x1, blocking collectives, local(): all_k = lax.all_gather(kvec.astype(F32), 'waves', axis=1, tiled=True)  4.58 us
    ppermute x1, starting transfers between devices, local(): lax.ppermute(hm3, 'atoms', backward)  4.49 us
  transfers between devices with their start and end apart: 5, of which 1 were waited for; matrix products, arithmetic and copies ran while one was open for 6% of the time, Pallas kernels for 19%

commit v1 on v0

v1 whole, which is shorter than its diff:
```python
import functools
import math

import jax
import jax.numpy as jnp
from jax import lax
from jax.experimental import pallas as pl
from jax.experimental.pallas import tpu as pltpu
from jax.sharding import PartitionSpec as P

BLOCK = 128
MSG_SCALE = 0.125
GAIN_TOP = 20.0
SIDE = 5
BASE = 2 * SIDE + 1
HALF = (BASE * BASE + 1) // 2
BATCH = 4
F32 = jnp.float32
BF16 = jnp.bfloat16
VMEM = pl.BlockSpec(memory_space=pltpu.VMEM)
SMEM = pl.BlockSpec(memory_space=pltpu.SMEM)
NT = (((1,), (1,)), ((), ()))
TN = (((0,), (0,)), ((), ()))
DMA = pltpu.SemaphoreType.DMA


def phase_rows(ta, tb_ref, pair, held):
    half = tb_ref.shape[0] // 2
    cb = tb_ref[pl.ds(pair, 1), :].astype(BF16)
    sb = tb_ref[pl.ds(half + pair, 1), :].astype(BF16)
    return ta * cb, ta * sb


def groups_of(count):
    return [(i, min(4, count - i)) for i in range(0, count, 4)]


MESH = pl.DeviceIdType.MESH


def meet(peers):
    barrier = pltpu.get_barrier_semaphore()
    for peer in peers:
        pl.semaphore_signal(barrier, inc=1, device_id=peer, device_id_type=MESH)
    pl.semaphore_wait(barrier, len(peers))


def others(axis):
    count = lax.axis_size(axis)
    me = lax.axis_index(axis)
    return [{axis: lax.rem(me + d, count)} for d in range(1, count)]


def send(src, dst, sends, receives, slot, peer):
    copy = pltpu.make_async_remote_copy(
        src_ref=src,
        dst_ref=dst,
        send_sem=sends.at[slot],
        recv_sem=receives.at[slot],
        device_id=peer,
        device_id_type=MESH,
    )
    copy.start()
    return copy


def structure_kernel(
    pairs, ta_ref, tb_ref, h_ref, pos_ref, hm_ref, k_ref, out_ref, near_ref, ext_ref, allk_ref, sends, receives
):
    a = ta_ref.shape[0]
    nblocks = pos_ref.shape[0]
    regions = lax.axis_size("atoms")
    here = lax.axis_index("atoms")
    wave = lax.axis_index("waves")
    right = {"atoms": lax.rem(here + 1, regions)}
    left = {"atoms": lax.rem(here + regions - 1, regions)}
    waves = others("waves")
    meet([left, right] + waves)
    copies = []
    for side, peer in ((0, right), (2, left)):
        place = pl.ds(side * nblocks, nblocks)
        copies.append(send(hm_ref, ext_ref.at[place], sends, receives, len(copies), peer))
        copies.append(send(pos_ref, near_ref.at[place], sends, receives, len(copies), peer))
    for peer in waves:
        copies.append(send(k_ref, allk_ref.at[wave], sends, receives, len(copies), peer))
    ext_ref[nblocks : 2 * nblocks] = hm_ref[...]
    near_ref[nblocks : 2 * nblocks] = pos_ref[...]
    allk_ref[wave] = k_ref[...]

    ta = ta_ref[...]
    h = h_ref[...]
    for first, size in groups_of(pairs):
        cs, ss = zip(*[phase_rows(ta, tb_ref, first + i, pairs) for i in range(size)])
        rows = slice(first * a, (first + size) * a)
        c = lax.dot_general(jnp.concatenate(cs, 0), h, NT, preferred_element_type=F32)
        s = lax.dot_general(jnp.concatenate(ss, 0), h, NT, preferred_element_type=F32)
        out_ref[rows, :] = jnp.concatenate([c, s], 1).astype(BF16)
    c = lax.dot_general(tb_ref[...].astype(BF16), h, NT, preferred_element_type=F32)
    out_ref[pairs * a : (pairs + 1) * a, :] = jnp.concatenate([c, jnp.zeros_like(c)], 1).astype(BF16)
    rest = out_ref.shape[0] - (pairs + 1) * a
    if rest:
        out_ref[(pairs + 1) * a :, :] = jnp.zeros((rest, out_ref.shape[1]), BF16)
    for copy in copies:
        copy.wait()


def exchange_kernel(
    scale_x,
    scale,
    a,
    idx_ref,
    live_ref,
    factor_ref,
    p_ref,
    q_ref,
    same_ref,
    cross_ref,
    own_ref,
    near_ref,
    hm_ref,
    out_ref,
    msg_ref,
    inbox,
    sends,
    receives,
    sends2,
    receives2,
):
    here = lax.axis_index("atoms")
    peers = others("atoms")
    meet(peers)
    copies = [
        send(factor_ref.at[peer["atoms"]], inbox.at[d], sends, receives, d, peer) for d, peer in enumerate(peers)
    ]
    blocks = own_ref.shape[0]
    early = blocks // 2
    short_blocks(scale_x, 0, early, idx_ref, live_ref, own_ref, near_ref, hm_ref, msg_ref)
    for copy in copies:
        copy.wait()
    total = factor_ref[here].astype(F32)
    for d in range(len(peers)):
        total = total + inbox[d].astype(F32)
    total = total * scale
    half = a // 2
    parts = []
    for row in range(0, total.shape[0], a):
        parts += [total[row + half : row + a], total[row : row + half]]
    partner = jnp.concatenate(parts, 0)
    high = lax.Precision.HIGHEST
    mixed = jnp.dot(total, same_ref[...], precision=high, preferred_element_type=F32)
    crossed = jnp.dot(partner, cross_ref[...], precision=high, preferred_element_type=F32)
    out_ref[here] = (p_ref[...] * mixed + q_ref[...] * crossed).astype(BF16)
    copies = [
        send(out_ref.at[here], out_ref.at[here], sends2, receives2, d, peer) for d, peer in enumerate(peers)
    ]
    short_blocks(scale_x, early, blocks, idx_ref, live_ref, own_ref, near_ref, hm_ref, msg_ref)
    for copy in copies:
        copy.wait()


def finish_kernel(
    pairs,
    scale,
    count_ref,
    ta_ref,
    tb_ref,
    g_ref,
    h_ref,
    mine_ref,
    first_ref,
    second_ref,
    out_ref,
    msg_ref,
    pot_ref,
    sends,
    receives,
):
    wave = lax.axis_index("waves")
    peers = others("waves")
    count = len(peers)
    meet(peers)
    msg_ref[wave] = mine_ref[...]
    copies = [
        send(mine_ref, msg_ref.at[wave], sends, receives, d, peer) for d, peer in enumerate(peers)
    ]
    a = ta_ref.shape[0]
    ta = ta_ref[...]
    rows = tb_ref.shape[0]
    acc = lax.dot_general(
        g_ref[pairs * a : pairs * a + rows, 0:64], tb_ref[...].astype(BF16), TN, preferred_element_type=F32
    )
    for first, size in groups_of(pairs):
        cs, ss = zip(*[phase_rows(ta, tb_ref, first + i, pairs) for i in range(size)])
        g = g_ref[first * a : (first + size) * a, :]
        acc += lax.dot_general(g[:, 0:64], jnp.concatenate(cs, 0), TN, preferred_element_type=F32)
        acc += lax.dot_general(g[:, 64:128], jnp.concatenate(ss, 0), TN, preferred_element_type=F32)
    pot_ref[wave] = (acc * scale).astype(BF16)
    copies += [
        send(pot_ref.at[wave], pot_ref.at[wave], sends, receives, count + d, peer) for d, peer in enumerate(peers)
    ]
    for copy in copies:
        copy.wait()
    h = h_ref[...]
    pot = pot_ref[0].astype(F32)
    for w in range(1, pot_ref.shape[0]):
        pot = pot + pot_ref[w].astype(F32)
    msg = jnp.concatenate(
        [msg_ref[w, b] for w in range(msg_ref.shape[0]) for b in range(msg_ref.shape[1])], 1
    )
    z = jnp.concatenate([h, msg, pot.astype(BF16)], 0)
    hidden = jnp.dot(first_ref[...], z, preferred_element_type=F32)
    hidden = (hidden * jax.nn.sigmoid(hidden)).astype(BF16)
    out = h.astype(F32) + jnp.dot(second_ref[...], hidden, preferred_element_type=F32)
    atom = lax.broadcasted_iota(jnp.int32, out.shape, 1)
    out_ref[...] = jnp.where(atom < count_ref[0] * BLOCK, out, 0.0).astype(BF16)


def short_blocks(scale_x, begin, end, idx_ref, live_ref, own_ref, near_ref, hm_ref, out_ref):
    steps = idx_ref.shape[0] // BATCH

    def block_step(b, _):
        own = own_ref[b]
        cols = [jnp.broadcast_to(own[:, d : d + 1], (BLOCK, BLOCK)) for d in range(3)]

        def slot_step(step, acc):
            weights, mapped = [], []
            for u in range(BATCH):
                s = step * BATCH + u
                n = idx_ref[s, b]
                near = near_ref[n]
                total = None
                for d in (1, 2, 0):
                    diff = cols[d] - near[d : d + 1, :]
                    diff = diff - jnp.round(diff)
                    if d == 0:
                        diff = diff * scale_x
                    total = diff * diff if total is None else total + diff * diff
                weights.append(jnp.exp2(total * (-2.0 * math.log2(math.e))).astype(BF16))
                mapped.append(hm_ref[n] * live_ref[s, b].astype(BF16))
            return acc + lax.dot_general(
                jnp.concatenate(mapped, 1), jnp.concatenate(weights, 1), NT, preferred_element_type=F32
            )

        acc = lax.fori_loop(0, steps, slot_step, jnp.zeros((hm_ref.shape[1], BLOCK), F32))
        out_ref[b] = (acc * MSG_SCALE).astype(BF16)
        return 0

    lax.fori_loop(begin, end, block_step, 0)


def call(kernel, ident, shapes, specs, scratch, *args):
    return pl.pallas_call(
        kernel,
        out_shape=[jax.ShapeDtypeStruct(shape, dtype) for shape, dtype in shapes],
        in_specs=specs,
        out_specs=[VMEM] * len(shapes),
        scratch_shapes=scratch,
        compiler_params=pltpu.CompilerParams(
            vmem_limit_bytes=48 * 1024 * 1024, collective_id=ident, has_side_effects=True
        ),
    )(*args)


def coefficients(kvec, regions, pairs, padded, first, here, owned, chans):
    top = 2 * regions
    k = jnp.where(kvec[0:1] < 0, -kvec, kvec)
    code = k[1] * BASE + k[2]
    n = jnp.abs(code) - first
    onehot_a = (jnp.arange(top + 1, dtype=F32)[:, None] == k[0][None, :]).astype(BF16)
    which = jnp.arange(pairs, dtype=F32)[:, None] == n[None, :]
    up = (which & (code >= 0)[None, :]).astype(BF16)
    down = (which & (code < 0)[None, :]).astype(BF16)
    m1 = lax.dot_general(up, onehot_a, NT, preferred_element_type=F32)
    m2 = lax.dot_general(down, onehot_a, NT, preferred_element_type=F32)
    b = jnp.arange(pairs, dtype=F32) + first
    ky = jnp.floor((b + SIDE) / BASE)
    kz = b - ky * BASE
    kx = jnp.arange(top + 1, dtype=F32) / regions
    gain = GAIN_TOP / (4.0 + (kx * kx)[None, :] + (ky * ky + kz * kz)[:, None])
    p = gain * (m1 + m2)
    q = gain * (m2 - m1)
    main_p, main_q = p[:, 1:], q[:, 1:]
    a = 2 * top
    p_rows = jnp.concatenate([main_p, main_p], 1).reshape(-1)
    q_cos = jnp.concatenate([main_q, -main_q], 1).reshape(-1)
    extra = jnp.pad(p[:, 0], (0, a // 2 - pairs))
    extra = jnp.concatenate([extra, extra])
    rest = (padded - pairs - 1) * a
    p_cos = jnp.concatenate([p_rows, extra, jnp.zeros((rest,), F32)])
    p_sin = jnp.concatenate([p_rows, jnp.zeros((a + rest,), F32)])
    q_cos = jnp.pad(q_cos, (0, a + rest))
    p_cos, p_sin, q_cos = [lax.dynamic_slice_in_dim(x, here * owned, owned, 0) for x in (p_cos, p_sin, q_cos)]
    wide = lambda x, y: jnp.concatenate(
        [jnp.broadcast_to(v[:, None], (owned, chans)) for v in (x, y)], 1
    )
    return wide(p_cos, p_sin), wide(q_cos, -q_cos)


def local(
    features,
    coords,
    neighbours,
    live_slots,
    block_count,
    kvec,
    msg_weight,
    filter_weight,
    mlp_in,
    mlp_out,
):
    chans, width = features.shape
    nblocks = width // BLOCK
    regions = lax.axis_size("atoms")
    groups = lax.axis_size("waves")
    here = lax.axis_index("atoms")
    wave = lax.axis_index("waves")
    total = regions * width
    waves_total = kvec.shape[1] * groups
    top = 2 * regions
    a = 2 * top
    pairs = -(-HALF // groups)
    padded = -(-(pairs + 1) // regions) * regions
    first = (wave * pairs).astype(F32)

    h = features
    live = jnp.arange(width, dtype=jnp.int32) < block_count[0] * BLOCK
    masked = jnp.where(live[None, :], h, jnp.zeros_like(h))

    hm = jnp.dot(msg_weight[0], h, preferred_element_type=F32).astype(BF16)
    hm3 = hm.reshape(chans, nblocks, BLOCK).transpose(1, 0, 2)
    pos3 = coords.reshape(3, nblocks, BLOCK).transpose(1, 0, 2)

    def turns(t, quarter):
        t = t - jnp.round(t)
        return jnp.cos((2.0 * math.pi) * (t - quarter))

    quarter = jnp.array([0.0, 0.25], F32)[:, None, None]
    ka = jnp.arange(1, top + 1, dtype=F32)
    ta = turns((ka[:, None] * coords[0][None, :])[None], quarter).reshape(a, width).astype(BF16)
    b = jnp.arange(top, dtype=F32) + first
    ky = jnp.floor((b + SIDE) / BASE)
    kz = b - ky * BASE
    tb = turns((ky[:, None] * coords[1][None, :] + kz[:, None] * coords[2][None, :])[None], quarter)
    tb = tb.reshape(a, width)

    copies = 4 + groups - 1
    factor, near, hm_ext, all_k = call(
        functools.partial(structure_kernel, pairs),
        0,
        [
            ((padded * a, 2 * chans), BF16),
            ((3 * nblocks, 3, BLOCK), F32),
            ((3 * nblocks, chans, BLOCK), BF16),
            ((groups,) + kvec.shape, F32),
        ],
        [VMEM] * 6,
        [DMA((copies,)), DMA((copies,))],
        ta,
        tb,
        masked,
        pos3,
        hm3,
        kvec.astype(F32),
    )
    all_k = all_k.transpose(1, 0, 2).reshape(kvec.shape[0], -1)

    source = neighbours // nblocks
    offset = (source - here) % regions
    which = jnp.where(offset == 0, 1, jnp.where(offset == 1, 2, 0))
    ext_index = which * nblocks + neighbours % nblocks
    mine = nblocks // groups
    slots = neighbours.shape[0]
    extra = -slots % BATCH
    start = wave * mine
    idx = jnp.pad(lax.dynamic_slice_in_dim(ext_index, start, mine, 1), ((0, extra), (0, 0)))
    used = jnp.pad(lax.dynamic_slice_in_dim(live_slots, start, mine, 1), ((0, extra), (0, 0))).astype(F32)
    own = lax.dynamic_slice_in_dim(pos3, start, mine, 0).transpose(0, 2, 1)
    owned = padded * a // regions
    p, q = coefficients(all_k, regions, pairs, padded, first, here, owned, chans)
    mixing = filter_weight[0]
    zero = jnp.zeros_like(mixing)
    same = jnp.block([[mixing, zero], [zero, mixing]])
    cross = jnp.block([[zero, mixing], [mixing, zero]])
    peers = regions - 1
    filtered, msg = call(
        functools.partial(exchange_kernel, float(regions), 1.0 / math.sqrt(total), a),
        1,
        [((regions, owned, 2 * chans), BF16), ((mine, chans, BLOCK), BF16)],
        [SMEM] * 2 + [VMEM] * 8,
        [pltpu.VMEM((peers, owned, 2 * chans), BF16)] + [DMA((peers,))] * 4,
        idx,
        used,
        factor.reshape(regions, owned, 2 * chans),
        p,
        q,
        same,
        cross,
        own,
        near,
        hm_ext,
    )
    peers = groups - 1
    return call(
        functools.partial(finish_kernel, pairs, 1.0 / math.sqrt(waves_total)),
        2,
        [((chans, width), BF16)],
        [SMEM] + [VMEM] * 7,
        [pltpu.VMEM((groups, mine, chans, BLOCK), BF16), pltpu.VMEM((groups, chans, width), BF16)]
        + [DMA((2 * peers,))] * 2,
        block_count,
        ta,
        tb,
        filtered.reshape(padded * a, 2 * chans),
        h,
        msg,
        mlp_in[0],
        mlp_out[0],
    )[0]


def solution(mesh):
    in_specs = (
        P(None, "atoms"),
        P(None, "atoms"),
        P(None, "atoms"),
        P(None, "atoms"),
        P("atoms"),
        P(None, "waves"),
        P(),
        P(),
        P(),
        P(),
    )
    out_specs = P(None, "atoms")
    return jax.shard_map(local, mesh=mesh, in_specs=in_specs, out_specs=out_specs, check_vma=False)
```

time: 131 us -> 71.7 us (0.55)
  the two profiles are of different devices: /device:TPU:0 before, /device:TPU:30 now
where the time goes in v1:
time: 71.7 us; the launch traced here: 71.1 us
  Pallas kernels  51.9 us (72%)
  local copies, waits for them, and re-layouts  9.69 us (14%)
  other arithmetic  7.74 us (11%)
  between operations  0.96 us (1%)
  matrix products  0.82 us (1%)
    pallas_call x3, Pallas kernels, call(): pl.pallas_call(kernel, out_shape=[jax.ShapeDtypeStruct(shape, dtype) for...  51.9 us
    unnamed x45, local copies, waits for them, and re-layouts  6.87 us
    cos x1, other arithmetic, turns(): return jnp.cos(2.0 * math.pi * (t - quarter))  3.43 us

profile of v1, /device:TPU:30, one launch (start us, length us, event | category | flops | bytes accessed | tf_op | source)
XLA Modules:
  0.0 71.1 jit_solution(6007548950691320715)
XLA Ops:
  0.7 0.0 copy-start.17
  0.7 0.6 multiply_add_fusion
  1.3 0.5 multiply_add_fusion.1
  1.8 0.1 sub.89
  1.9 0.1 sub.90
  2.0 0.1 copy.29
  2.1 0.6 pad_convert_fusion.live_ref
  2.7 0.1 copy-done.15
  2.8 0.1 copy.20
  2.9 0.1 fusion.20
  3.0 0.0 copy-start.11
  3.1 0.6 pad.18.idx_ref
  3.7 0.1 copy-done.11
  3.8 0.0 copy-start.12
  3.8 0.7 %copy-done.14 = s32[3,2048]{1,0:T(4,128)S(1)} copy-done((s32[3,2048]{1,0:T(4,128)S(1)}, s32[3,2048]{1,0:T(4,128)}, u32[]{:S(2)}) %copy-start.14) | copy-done | bytes 24600
  4.6 0.6 convert_element_type.26.k_ref
  5.2 0.0 copy-done.12
  5.2 0.7 %copy.28 = bf16[1,128,192]{2,1,0:T(8,128)(2,1)} copy(bf16[1,128,192]{1,2,0:T(8,128)(2,1)S(1)} %copy-done.12) | data formatting | bytes 98304 | tf_op args[8]
  5.9 0.0 copy-done.13
  5.9 0.1 fusion.25
  6.0 0.0 copy-start.1
  6.0 0.1 round-nearest-even_subtract_fusion
  6.2 0.1 round-nearest-even_subtract_fusion.1
  6.3 0.7 %copy-done.1 = bf16[64,2048]{1,0:T(8,128)(2,1)S(1)} copy-done((bf16[64,2048]{1,0:T(8,128)(2,1)S(1)}, bf16[64,2048]{1,0:T(8,128)(2,1)}, u32[]{:S(2)}) %copy-start.1) | copy-done | bytes 262168
  7.0 3.4 %fusion.4 = (f32[64,2048]{1,0:T(8,128)S(1)}, bf16[64,2048]{1,0:T(8,128)(2,1)S(1)}) fusion(f32[32,2048]{1,0:T(8,128)S(1)} %round-nearest-even_subtract_fusion, f32[64]{0:T(128)S(1)} %sub.90, f32[32,2048]{1,0:T(8,128)S(1)} %round-nearest-even_subtract_fusion.1), kind=kLoop, calls=%fused_computation.7 | loop fusion | flops 655360 | bytes 1310976 | tf_op jit(solution)/shard_map/cos | solution.py:335
  10.4 0.0 copy-done
  10.5 0.2 fusion
  10.7 0.1 copy.32
  10.7 0.4 copy.25
  11.1 0.9 %copy.27.pos_ref = f32[16,3,128]{2,1,0:T(4,128)} copy(f32[16,3,128]{1,2,0:T(8,128)S(1)} %bitcast.52) | data formatting | bytes 49152 | tf_op jit(solution)/shard_map/transpose | solution.py:331
  12.1 0.7 %copy-done.3 = f32[16,3,128]{2,1,0:T(4,128)S(1)} copy-done((f32[16,3,128]{2,1,0:T(4,128)S(1)}, f32[16,3,128]{2,1,0:T(4,128)}, u32[]{:S(2)}) %copy-start.3) | copy-done | bytes 24600
  12.8 0.0 copy-done.4
  12.8 9.2 %shard_map.109 = (bf16[2048,128]{1,0:T(8,128)(2,1)S(1)}, f32[48,3,128]{2,1,0:T(4,128)S(1)}, bf16[48,64,128]{2,1,0:T(8,128)(2,1)S(1)}, f32[2,3,2048]{2,1,0:T(4,128)S(1)}) custom-call(bf16[64,2048]{1,0:T(8,128)(2,1)S(1)} %get-tuple-element.37.ta_ref, f32[64,2048]{1,0:T(8,128)S(1)} %get-tuple-element.36.tb_ref, ...), custom_call_target="tpu_custom_call" | custom-call | tf_op jit(solution)/shard_map/pallas_call | solution.py:252
  22.1 0.0 copy-start.6
  22.1 0.6 copy-done.6
  22.7 0.6 copy-done.5
  23.3 0.1 compare_reduce_fusion.2
  23.4 0.9 %negate_select_fusion = f32[3,4096]{1,0:T(4,128)S(1)} fusion(f32[3,4096]{1,0:T(4,128)} %bitcast.50, pred[4096]{0:T(1024)(128)(4,1)S(1)} %lt.57), kind=kLoop, calls=%fused_computation.26 | loop fusion | flops 24576 | bytes 102400 | tf_op jit(solution)/shard_map/jit(_where)/select_n | solution.py:266
  24.3 0.1 compare_reduce_fusion
  24.5 0.3 fusion.1
  24.8 0.4 copy-done.18
  25.2 0.3 add_divide_fusion
  25.5 0.1 fusion.24
  25.5 0.1 pad_maximum_fusion.5
  25.6 0.1 reshape.183
  25.7 0.1 fusion.23
  25.8 0.1 slice_reduce_fusion
  25.9 0.1 slice.54
  26.0 0.1 pad_maximum_fusion.4
  26.0 0.1 reshape.182
  26.1 0.1 pad_dynamic-slice_fusion.1
  26.2 0.1 concatenate.36
  26.3 0.1 dynamic_slice.18
  26.4 0.1 broadcast_in_dim.38
  26.4 0.1 broadcast_in_dim.39
  26.5 0.1 pad_maximum_fusion.p_ref
  26.6 0.1 broadcast_in_dim.41
  26.7 0.1 broadcast_in_dim.40
  26.8 0.0 copy-start.7
  26.8 0.1 pad_maximum_fusion.1.q_ref
  26.9 0.8 %copy-done.7 = f32[48,3,128]{2,1,0:T(4,128)S(1)} copy-done((f32[48,3,128]{2,1,0:T(4,128)S(1)}, f32[48,3,128]{2,1,0:T(4,128)}, u32[]{:S(2)}) %copy-start.7) | copy-done | bytes 73752
  27.7 30.3 %shard_map.110 = (bf16[16,128,128]{2,1,0:T(8,128)(2,1)S(1)}, bf16[8,64,128]{2,1,0:T(8,128)(2,1)S(1)}) custom-call(s32[28,8]{1,0:T(8,128)S(1)} %copy-done.9, f32[28,8]{1,0:T(8,128)S(1)} %copy-done.8, bf16[16,128,128]{2,1,0:T(8,128)(2,1)S(1)} %bitcast.46, f32[128,128]{1,0:T(8,128)S(1)} %pad_maximum_fusion.p_ref, f32[128,128]{1,0:T(8,128)S(1)} %pad_maximum_fusion.1.q_ref, ...), custom_call_target="tpu_custom_call" | custom-call | tf_op jit(solution)/shard_map/pallas_call | solution.py:252
  58.0 12.4 %shard_map.111 = bf16[64,2048]{1,0:T(8,128)(2,1)S(1)} custom-call(s32[1]{0:T(128)S(6)} %copy.34.count_ref, bf16[64,2048]{1,0:T(8,128)(2,1)S(1)} %get-tuple-element.37.ta_ref, f32[64,2048]{1,0:T(8,128)S(1)} %get-tuple-element.36.tb_ref, bf16[2048,128]{1,0:T(8,128)(2,1)S(1)} %bitcast.47, bf16[64,2048]{1,0:T(8,128)(2,1)S(1)} %copy-done.1, ...), custom_call_target="tpu_custom_call" | custom-call | tf_op jit(solution)/shard_map/pallas_call | solution.py:252
  70.4 0.7 copy.35
  (35 shorter events, 0.3 us)
Async XLA Ops:
  0.0 10.4 %copy-start = (bf16[1,64,64]{2,1,0:T(8,128)(2,1)S(1)}, bf16[1,64,64]{2,1,0:T(8,128)(2,1)}, u32[]{:S(2)}) copy-start(bf16[1,64,64]{2,1,0:T(8,128)(2,1)} %param.17) | copy-start | bytes 24580
  0.7 1.1 %copy-start.17 = (f32[2]{0:T(128)S(1)}, f32[2]{0:T(128)}, u32[]{:S(2)}) copy-start(f32[2]{0:T(128)} %constant.89.clone) | copy-start | bytes 28
  1.3 0.7 copy-start.16
  2.1 0.7 copy-start.15
  3.0 0.8 %copy-start.11 = (f32[3,2048]{1,0:T(4,128)S(1)}, f32[3,2048]{1,0:T(4,128)}, u32[]{:S(2)}) copy-start(f32[3,2048]{1,0:T(4,128)} %param.12) | copy-start | bytes 73732
  3.8 0.8 %copy-start.14 = (s32[3,2048]{1,0:T(4,128)S(1)}, s32[3,2048]{1,0:T(4,128)}, u32[]{:S(2)}) copy-start(s32[3,2048]{1,0:T(4,128)} %param.16) | copy-start | bytes 73732
  3.8 1.3 %copy-start.12 = (bf16[1,128,192]{1,2,0:T(8,128)(2,1)S(1)}, bf16[1,128,192]{1,2,0:T(8,128)(2,1)}, u32[]{:S(2)}) copy-start(bf16[1,128,192]{1,2,0:T(8,128)(2,1)} %param.19) | copy-start | bytes 147460
  5.2 0.8 %copy-start.13 = (f32[1,64,64]{2,1,0:T(8,128)S(1)}, f32[1,64,64]{2,1,0:T(8,128)}, u32[]{:S(2)}) copy-start(f32[1,64,64]{2,1,0:T(8,128)} %param.18) | copy-start | bytes 49156
  6.0 1.0 %copy-start.1 = (bf16[64,2048]{1,0:T(8,128)(2,1)S(1)}, bf16[64,2048]{1,0:T(8,128)(2,1)}, u32[]{:S(2)}) copy-start(bf16[64,2048]{1,0:T(8,128)(2,1)} %h_ref.1) | copy-start | bytes 786436
  12.1 0.8 %copy-start.3 = (f32[16,3,128]{2,1,0:T(4,128)S(1)}, f32[16,3,128]{2,1,0:T(4,128)}, u32[]{:S(2)}) copy-start(f32[16,3,128]{2,1,0:T(4,128)} %copy.27.pos_ref) | copy-start | bytes 73732
  12.1 0.8 %copy-start.4 = (f32[3,2048]{1,0:T(4,128)S(1)}, f32[3,2048]{1,0:T(4,128)}, u32[]{:S(2)}) copy-start(f32[3,2048]{1,0:T(4,128)} %convert_element_type.26.k_ref) | copy-start | bytes 73732
  22.1 0.6 copy-start.6
  22.7 0.6 copy-start.5
  24.5 0.7 copy-start.18
  24.5 0.7 copy-start.19
  26.8 0.9 %copy-start.7 = (f32[48,3,128]{2,1,0:T(4,128)S(1)}, f32[48,3,128]{2,1,0:T(4,128)}, u32[]{:S(2)}) copy-start(f32[48,3,128]{2,1,0:T(4,128)} %copy-done.6) | copy-start | bytes 221188
  26.8 0.9 %copy-start.8 = (f32[28,8]{1,0:T(8,128)S(1)}, f32[28,8]{1,0:T(8,128)}, u32[]{:S(2)}) copy-start(f32[28,8]{1,0:T(8,128)} %pad_convert_fusion.live_ref) | copy-start | bytes 2692
  26.8 0.9 %copy-start.9 = (s32[28,8]{1,0:T(8,128)S(1)}, s32[28,8]{1,0:T(8,128)}, u32[]{:S(2)}) copy-start(s32[28,8]{1,0:T(8,128)} %pad.18.idx_ref) | copy-start | bytes 2692
  27.7 30.3 %copy-start.2 = (bf16[1,128,192]{2,1,0:T(8,128)(2,1)S(1)}, bf16[1,128,192]{2,1,0:T(8,128)(2,1)}, u32[]{:S(2)}) copy-start(bf16[1,128,192]{2,1,0:T(8,128)(2,1)} %copy.28) | copy-start | bytes 147460
  27.7 30.3 %copy-start.10 = (bf16[1,64,128]{2,1,0:T(8,128)(2,1)S(1)}, bf16[1,64,128]{2,1,0:T(8,128)(2,1)}, u32[]{:S(2)}) copy-start(bf16[1,64,128]{2,1,0:T(8,128)(2,1)} %param.20) | copy-start | bytes 49156

commit v2 on v1

--- a/solution.py
+++ b/solution.py
@@ -14,7 +14,7 @@
 SIDE = 5
 BASE = 2 * SIDE + 1
 HALF = (BASE * BASE + 1) // 2
-BATCH = 4
+BATCH = 7
 F32 = jnp.float32
 BF16 = jnp.bfloat16
 VMEM = pl.BlockSpec(memory_space=pltpu.VMEM)
@@ -238,11 +238,11 @@
                 weights.append(jnp.exp2(total * (-2.0 * math.log2(math.e))).astype(BF16))
                 mapped.append(hm_ref[n] * live_ref[s, b].astype(BF16))
             return acc + lax.dot_general(
-                jnp.concatenate(mapped, 1), jnp.concatenate(weights, 1), NT, preferred_element_type=F32
+                jnp.concatenate(weights, 1), jnp.concatenate(mapped, 1), NT, preferred_element_type=F32
             )
 
-        acc = lax.fori_loop(0, steps, slot_step, jnp.zeros((hm_ref.shape[1], BLOCK), F32))
-        out_ref[b] = (acc * MSG_SCALE).astype(BF16)
+        acc = lax.fori_loop(0, steps, slot_step, jnp.zeros((BLOCK, hm_ref.shape[1]), F32))
+        out_ref[b] = (acc * MSG_SCALE).T.astype(BF16)
         return 0
 
     lax.fori_loop(begin, end, block_step, 0)

time: 71.7 us -> 72 us (level)
  no operation moved by 1% of the time
where the time goes in v2:
time: 72 us; the launch traced here: 71.4 us
  Pallas kernels  52.2 us (72%)
  local copies, waits for them, and re-layouts  9.69 us (13%)
  other arithmetic  7.74 us (11%)
  between operations  0.96 us (1%)
  matrix products  0.82 us (1%)
    pallas_call x3, Pallas kernels, call(): pl.pallas_call(kernel, out_shape=[jax.ShapeDtypeStruct(shape, dtype) for...  52.2 us
    unnamed x45, local copies, waits for them, and re-layouts  6.87 us
    cos x1, other arithmetic, turns(): return jnp.cos(2.0 * math.pi * (t - quarter))  3.43 us

profile of v2, /device:TPU:30, one launch (start us, length us, event | category | flops | bytes accessed | tf_op | source)
XLA Modules:
  0.0 71.4 jit_solution(15134497811001898731)
XLA Ops:
  0.7 0.0 copy-start.17
  0.7 0.6 multiply_add_fusion
  1.3 0.5 multiply_add_fusion.1
  1.8 0.1 sub.89
  1.9 0.1 sub.90
  2.0 0.1 copy.29
  2.1 0.6 pad_convert_fusion.live_ref
  2.7 0.1 copy-done.15
  2.8 0.1 copy.20
  2.9 0.1 fusion.20
  3.0 0.0 copy-start.11
  3.1 0.6 pad.18.idx_ref
  3.7 0.1 copy-done.11
  3.8 0.0 copy-start.12
  3.8 0.7 %copy-done.14 = s32[3,2048]{1,0:T(4,128)S(1)} copy-done((s32[3,2048]{1,0:T(4,128)S(1)}, s32[3,2048]{1,0:T(4,128)}, u32[]{:S(2)}) %copy-start.14) | copy-done | bytes 24600
  4.6 0.6 convert_element_type.26.k_ref
  5.2 0.0 copy-done.12
  5.2 0.7 %copy.28 = bf16[1,128,192]{2,1,0:T(8,128)(2,1)} copy(bf16[1,128,192]{1,2,0:T(8,128)(2,1)S(1)} %copy-done.12) | data formatting | bytes 98304 | tf_op args[8]
  5.9 0.0 copy-done.13
  5.9 0.1 fusion.25
  6.0 0.0 copy-start.1
  6.0 0.1 round-nearest-even_subtract_fusion
  6.2 0.1 round-nearest-even_subtract_fusion.1
  6.3 0.7 %copy-done.1 = bf16[64,2048]{1,0:T(8,128)(2,1)S(1)} copy-done((bf16[64,2048]{1,0:T(8,128)(2,1)S(1)}, bf16[64,2048]{1,0:T(8,128)(2,1)}, u32[]{:S(2)}) %copy-start.1) | copy-done | bytes 262168
  7.0 3.4 %fusion.4 = (f32[64,2048]{1,0:T(8,128)S(1)}, bf16[64,2048]{1,0:T(8,128)(2,1)S(1)}) fusion(f32[32,2048]{1,0:T(8,128)S(1)} %round-nearest-even_subtract_fusion, f32[64]{0:T(128)S(1)} %sub.90, f32[32,2048]{1,0:T(8,128)S(1)} %round-nearest-even_subtract_fusion.1), kind=kLoop, calls=%fused_computation.7 | loop fusion | flops 655360 | bytes 1310976 | tf_op jit(solution)/shard_map/cos | solution.py:335
  10.4 0.0 copy-done
  10.5 0.2 fusion
  10.7 0.1 copy.32
  10.7 0.4 copy.25
  11.1 0.9 %copy.27.pos_ref = f32[16,3,128]{2,1,0:T(4,128)} copy(f32[16,3,128]{1,2,0:T(8,128)S(1)} %bitcast.52) | data formatting | bytes 49152 | tf_op jit(solution)/shard_map/transpose | solution.py:331
  12.1 0.7 %copy-done.3 = f32[16,3,128]{2,1,0:T(4,128)S(1)} copy-done((f32[16,3,128]{2,1,0:T(4,128)S(1)}, f32[16,3,128]{2,1,0:T(4,128)}, u32[]{:S(2)}) %copy-start.3) | copy-done | bytes 24600
  12.8 0.0 copy-done.4
  12.8 9.2 %shard_map.109 = (bf16[2048,128]{1,0:T(8,128)(2,1)S(1)}, f32[48,3,128]{2,1,0:T(4,128)S(1)}, bf16[48,64,128]{2,1,0:T(8,128)(2,1)S(1)}, f32[2,3,2048]{2,1,0:T(4,128)S(1)}) custom-call(bf16[64,2048]{1,0:T(8,128)(2,1)S(1)} %get-tuple-element.37.ta_ref, f32[64,2048]{1,0:T(8,128)S(1)} %get-tuple-element.36.tb_ref, ...), custom_call_target="tpu_custom_call" | custom-call | tf_op jit(solution)/shard_map/pallas_call | solution.py:252
  22.1 0.0 copy-start.6
  22.1 0.6 copy-done.6
  22.7 0.6 copy-done.5
  23.3 0.1 compare_reduce_fusion.2
  23.4 0.9 %negate_select_fusion = f32[3,4096]{1,0:T(4,128)S(1)} fusion(f32[3,4096]{1,0:T(4,128)} %bitcast.50, pred[4096]{0:T(1024)(128)(4,1)S(1)} %lt.57), kind=kLoop, calls=%fused_computation.26 | loop fusion | flops 24576 | bytes 102400 | tf_op jit(solution)/shard_map/jit(_where)/select_n | solution.py:266
  24.3 0.1 compare_reduce_fusion
  24.5 0.3 fusion.1
  24.8 0.4 copy-done.18
  25.2 0.3 add_divide_fusion
  25.5 0.1 fusion.24
  25.5 0.1 pad_maximum_fusion.5
  25.6 0.1 reshape.183
  25.7 0.1 fusion.23
  25.8 0.1 slice_reduce_fusion
  25.9 0.1 slice.54
  26.0 0.1 pad_maximum_fusion.4
  26.0 0.1 reshape.182
  26.1 0.1 pad_dynamic-slice_fusion.1
  26.2 0.1 concatenate.36
  26.3 0.1 dynamic_slice.18
  26.4 0.1 broadcast_in_dim.38
  26.4 0.1 broadcast_in_dim.39
  26.5 0.1 pad_maximum_fusion.p_ref
  26.6 0.1 broadcast_in_dim.41
  26.7 0.1 broadcast_in_dim.40
  26.8 0.0 copy-start.7
  26.8 0.1 pad_maximum_fusion.1.q_ref
  26.9 0.8 %copy-done.7 = f32[48,3,128]{2,1,0:T(4,128)S(1)} copy-done((f32[48,3,128]{2,1,0:T(4,128)S(1)}, f32[48,3,128]{2,1,0:T(4,128)}, u32[]{:S(2)}) %copy-start.7) | copy-done | bytes 73752
  27.7 30.6 %shard_map.110 = (bf16[16,128,128]{2,1,0:T(8,128)(2,1)S(1)}, bf16[8,64,128]{2,1,0:T(8,128)(2,1)S(1)}) custom-call(s32[28,8]{1,0:T(8,128)S(1)} %copy-done.9, f32[28,8]{1,0:T(8,128)S(1)} %copy-done.8, bf16[16,128,128]{2,1,0:T(8,128)(2,1)S(1)} %bitcast.46, f32[128,128]{1,0:T(8,128)S(1)} %pad_maximum_fusion.p_ref, f32[128,128]{1,0:T(8,128)S(1)} %pad_maximum_fusion.1.q_ref, ...), custom_call_target="tpu_custom_call" | custom-call | tf_op jit(solution)/shard_map/pallas_call | solution.py:252
  58.3 12.4 %shard_map.111 = bf16[64,2048]{1,0:T(8,128)(2,1)S(1)} custom-call(s32[1]{0:T(128)S(6)} %copy.34.count_ref, bf16[64,2048]{1,0:T(8,128)(2,1)S(1)} %get-tuple-element.37.ta_ref, f32[64,2048]{1,0:T(8,128)S(1)} %get-tuple-element.36.tb_ref, bf16[2048,128]{1,0:T(8,128)(2,1)S(1)} %bitcast.47, bf16[64,2048]{1,0:T(8,128)(2,1)S(1)} %copy-done.1, ...), custom_call_target="tpu_custom_call" | custom-call | tf_op jit(solution)/shard_map/pallas_call | solution.py:252
  70.7 0.7 copy.35
  (35 shorter events, 0.3 us)
Async XLA Ops:
  0.0 10.4 %copy-start = (bf16[1,64,64]{2,1,0:T(8,128)(2,1)S(1)}, bf16[1,64,64]{2,1,0:T(8,128)(2,1)}, u32[]{:S(2)}) copy-start(bf16[1,64,64]{2,1,0:T(8,128)(2,1)} %param.17) | copy-start | bytes 24580
  0.7 1.1 %copy-start.17 = (f32[2]{0:T(128)S(1)}, f32[2]{0:T(128)}, u32[]{:S(2)}) copy-start(f32[2]{0:T(128)} %constant.89.clone) | copy-start | bytes 28
  1.3 0.7 copy-start.16
  2.1 0.7 copy-start.15
  3.0 0.8 %copy-start.11 = (f32[3,2048]{1,0:T(4,128)S(1)}, f32[3,2048]{1,0:T(4,128)}, u32[]{:S(2)}) copy-start(f32[3,2048]{1,0:T(4,128)} %param.12) | copy-start | bytes 73732
  3.8 0.8 %copy-start.14 = (s32[3,2048]{1,0:T(4,128)S(1)}, s32[3,2048]{1,0:T(4,128)}, u32[]{:S(2)}) copy-start(s32[3,2048]{1,0:T(4,128)} %param.16) | copy-start | bytes 73732
  3.8 1.3 %copy-start.12 = (bf16[1,128,192]{1,2,0:T(8,128)(2,1)S(1)}, bf16[1,128,192]{1,2,0:T(8,128)(2,1)}, u32[]{:S(2)}) copy-start(bf16[1,128,192]{1,2,0:T(8,128)(2,1)} %param.19) | copy-start | bytes 147460
  5.2 0.8 %copy-start.13 = (f32[1,64,64]{2,1,0:T(8,128)S(1)}, f32[1,64,64]{2,1,0:T(8,128)}, u32[]{:S(2)}) copy-start(f32[1,64,64]{2,1,0:T(8,128)} %param.18) | copy-start | bytes 49156
  6.0 1.0 %copy-start.1 = (bf16[64,2048]{1,0:T(8,128)(2,1)S(1)}, bf16[64,2048]{1,0:T(8,128)(2,1)}, u32[]{:S(2)}) copy-start(bf16[64,2048]{1,0:T(8,128)(2,1)} %h_ref.1) | copy-start | bytes 786436
  12.1 0.8 %copy-start.3 = (f32[16,3,128]{2,1,0:T(4,128)S(1)}, f32[16,3,128]{2,1,0:T(4,128)}, u32[]{:S(2)}) copy-start(f32[16,3,128]{2,1,0:T(4,128)} %copy.27.pos_ref) | copy-start | bytes 73732
  12.1 0.8 %copy-start.4 = (f32[3,2048]{1,0:T(4,128)S(1)}, f32[3,2048]{1,0:T(4,128)}, u32[]{:S(2)}) copy-start(f32[3,2048]{1,0:T(4,128)} %convert_element_type.26.k_ref) | copy-start | bytes 73732
  22.1 0.6 copy-start.6
  22.7 0.6 copy-start.5
  24.5 0.7 copy-start.18
  24.5 0.7 copy-start.19
  26.8 0.9 %copy-start.7 = (f32[48,3,128]{2,1,0:T(4,128)S(1)}, f32[48,3,128]{2,1,0:T(4,128)}, u32[]{:S(2)}) copy-start(f32[48,3,128]{2,1,0:T(4,128)} %copy-done.6) | copy-start | bytes 221188
  26.8 0.9 %copy-start.8 = (f32[28,8]{1,0:T(8,128)S(1)}, f32[28,8]{1,0:T(8,128)}, u32[]{:S(2)}) copy-start(f32[28,8]{1,0:T(8,128)} %pad_convert_fusion.live_ref) | copy-start | bytes 2692
  26.8 0.9 %copy-start.9 = (s32[28,8]{1,0:T(8,128)S(1)}, s32[28,8]{1,0:T(8,128)}, u32[]{:S(2)}) copy-start(s32[28,8]{1,0:T(8,128)} %pad.18.idx_ref) | copy-start | bytes 2692
  27.7 30.6 %copy-start.2 = (bf16[1,128,192]{2,1,0:T(8,128)(2,1)S(1)}, bf16[1,128,192]{2,1,0:T(8,128)(2,1)}, u32[]{:S(2)}) copy-start(bf16[1,128,192]{2,1,0:T(8,128)(2,1)} %copy.28) | copy-start | bytes 147460
  27.7 30.6 %copy-start.10 = (bf16[1,64,128]{2,1,0:T(8,128)(2,1)S(1)}, bf16[1,64,128]{2,1,0:T(8,128)(2,1)}, u32[]{:S(2)}) copy-start(bf16[1,64,128]{2,1,0:T(8,128)(2,1)} %param.20) | copy-start | bytes 49156

commit v3 on v1

--- a/solution.py
+++ b/solution.py
@@ -15,6 +15,8 @@
 BASE = 2 * SIDE + 1
 HALF = (BASE * BASE + 1) // 2
 BATCH = 4
+CHUNK = 256
+COS = [(-1.0) ** n * (2.0 * math.pi) ** (2 * n) / math.factorial(2 * n) for n in range(10)]
 F32 = jnp.float32
 BF16 = jnp.bfloat16
 VMEM = pl.BlockSpec(memory_space=pltpu.VMEM)
@@ -64,10 +66,38 @@
     return copy
 
 
+def cos_turns(u):
+    w = u * u
+    out = COS[-1] * w + COS[-2]
+    for c in COS[-3::-1]:
+        out = out * w + c
+    return out
+
+
+def cos_sin(t):
+    t = t - jnp.round(t)
+    shifted = t - 0.25
+    return cos_turns(t), cos_turns(shifted - jnp.round(shifted))
+
+
 def structure_kernel(
-    pairs, ta_ref, tb_ref, h_ref, pos_ref, hm_ref, k_ref, out_ref, near_ref, ext_ref, allk_ref, sends, receives
+    pairs,
+    coords_ref,
+    h_ref,
+    pos_ref,
+    hm_ref,
+    k_ref,
+    out_ref,
+    near_ref,
+    ext_ref,
+    allk_ref,
+    ta_ref,
+    tb_ref,
+    sends,
+    receives,
 ):
     a = ta_ref.shape[0]
+    top = a // 2
     nblocks = pos_ref.shape[0]
     regions = lax.axis_size("atoms")
     here = lax.axis_index("atoms")
@@ -87,6 +117,24 @@
     near_ref[nblocks : 2 * nblocks] = pos_ref[...]
     allk_ref[wave] = k_ref[...]
 
+    ka = lax.broadcasted_iota(jnp.int32, (top, CHUNK), 0).astype(F32)
+    b = ka + (wave * pairs).astype(F32)
+    ka = ka + 1.0
+    ky = jnp.floor((b + SIDE) * (1.0 / BASE) + 0.5 / BASE)
+    kz = b - ky * BASE
+
+    def table_step(index, _):
+        lanes = pl.ds(pl.multiple_of(index * CHUNK, CHUNK), CHUNK)
+        xyz = coords_ref[:, lanes]
+        ta = cos_sin(ka * xyz[0:1])
+        ta_ref[0:top, lanes] = ta[0].astype(BF16)
+        ta_ref[top:a, lanes] = ta[1].astype(BF16)
+        tb = cos_sin(ky * xyz[1:2] + kz * xyz[2:3])
+        tb_ref[0:top, lanes] = tb[0]
+        tb_ref[top:a, lanes] = tb[1]
+        return 0
+
+    lax.fori_loop(0, coords_ref.shape[1] // CHUNK, table_step, 0)
     ta = ta_ref[...]
     h = h_ref[...]
     for first, size in groups_of(pairs):
@@ -330,21 +378,8 @@
     hm3 = hm.reshape(chans, nblocks, BLOCK).transpose(1, 0, 2)
     pos3 = coords.reshape(3, nblocks, BLOCK).transpose(1, 0, 2)
 
-    def turns(t, quarter):
-        t = t - jnp.round(t)
-        return jnp.cos((2.0 * math.pi) * (t - quarter))
-
-    quarter = jnp.array([0.0, 0.25], F32)[:, None, None]
-    ka = jnp.arange(1, top + 1, dtype=F32)
-    ta = turns((ka[:, None] * coords[0][None, :])[None], quarter).reshape(a, width).astype(BF16)
-    b = jnp.arange(top, dtype=F32) + first
-    ky = jnp.floor((b + SIDE) / BASE)
-    kz = b - ky * BASE
-    tb = turns((ky[:, None] * coords[1][None, :] + kz[:, None] * coords[2][None, :])[None], quarter)
-    tb = tb.reshape(a, width)
-
     copies = 4 + groups - 1
-    factor, near, hm_ext, all_k = call(
+    factor, near, hm_ext, all_k, ta, tb = call(
         functools.partial(structure_kernel, pairs),
         0,
         [
@@ -352,11 +387,12 @@
             ((3 * nblocks, 3, BLOCK), F32),
             ((3 * nblocks, chans, BLOCK), BF16),
             ((groups,) + kvec.shape, F32),
+            ((a, width), BF16),
+            ((a, width), F32),
         ],
-        [VMEM] * 6,
+        [VMEM] * 5,
         [DMA((copies,)), DMA((copies,))],
-        ta,
-        tb,
+        coords,
         masked,
         pos3,
         hm3,

time: 71.7 us -> 66.8 us (0.932)
  other arithmetic: 7.74 us -> 4.12 us
  local copies, waits for them, and re-layouts: 9.69 us -> 8.55 us
    cos x1 -> x0, other arithmetic: 3.43 us -> none  [turns(): return jnp.cos(2.0 * math.pi * (t - quarter))]
    unnamed x45, local copies, waits for them, and re-layouts: 6.87 us -> 5.97 us
where the time goes in v3:
time: 66.8 us; the launch traced here: 66.4 us
  Pallas kernels  51.9 us (78%)
  local copies, waits for them, and re-layouts  8.55 us (13%)
  other arithmetic  4.12 us (6%)
  between operations  0.97 us (1%)
  matrix products  0.82 us (1%)
    pallas_call x3, Pallas kernels, call(): pl.pallas_call(kernel, out_shape=[jax.ShapeDtypeStruct(shape, dtype) for...  51.9 us
    unnamed x45, local copies, waits for them, and re-layouts  5.97 us

profile of v3, /device:TPU:30, one launch (start us, length us, event | category | flops | bytes accessed | tf_op | source)
XLA Modules:
  0.0 66.4 jit_solution(6100523707070560826)
XLA Ops:
  0.0 0.0 copy-start
  0.7 0.6 multiply_add_fusion
  1.3 0.5 multiply_add_fusion.1
  1.8 0.0 copy-done.17
  1.9 0.1 copy.28
  2.0 0.6 pad_convert_fusion.live_ref
  2.6 0.1 copy-done.16
  2.7 0.1 copy.22
  2.8 0.0 copy-start.15
  2.8 0.0 copy-start.13
  2.8 0.0 copy-start.14
  2.8 0.1 fusion.15
  2.9 0.0 copy-start.1
  2.9 0.6 pad.18.idx_ref
  3.5 0.0 copy-done.15
  3.6 0.6 convert_element_type.20.k_ref
  4.2 0.0 copy-done.13
  4.2 0.7 %copy.27 = bf16[1,128,192]{2,1,0:T(8,128)(2,1)} copy(bf16[1,128,192]{1,2,0:T(8,128)(2,1)S(1)} %copy-done.13) | data formatting | bytes 98304 | tf_op args[8]
  4.9 0.0 copy-done.14
  4.9 0.1 fusion.20
  5.0 0.0 copy-done.1
  5.1 0.0 copy-done
  5.1 0.2 fusion
  5.3 0.0 copy-start.3
  5.3 0.1 copy.31
  5.4 0.7 %copy-done.3 = f32[3,2048]{1,0:T(4,128)S(1)} copy-done((f32[3,2048]{1,0:T(4,128)S(1)}, f32[3,2048]{1,0:T(4,128)}, u32[]{:S(2)}) %copy-start.3) | copy-done | bytes 24600
  6.0 0.4 copy.19
  6.4 0.9 %copy.21.pos_ref = f32[16,3,128]{2,1,0:T(4,128)} copy(f32[16,3,128]{1,2,0:T(8,128)S(1)} %bitcast.35) | data formatting | bytes 49152 | tf_op jit(solution)/shard_map/transpose | solution.py:379
  7.4 0.7 %copy-done.4 = f32[3,2048]{1,0:T(4,128)S(1)} copy-done((f32[3,2048]{1,0:T(4,128)S(1)}, f32[3,2048]{1,0:T(4,128)}, u32[]{:S(2)}) %copy-start.4) | copy-done | bytes 24600
  8.1 0.0 copy-done.5
  8.1 0.0 copy-done.6
  8.1 9.2 %shard_map.100 = (bf16[2048,128]{1,0:T(8,128)(2,1)S(1)}, f32[48,3,128]{2,1,0:T(4,128)S(1)}, bf16[48,64,128]{2,1,0:T(8,128)(2,1)S(1)}, f32[2,3,2048]{2,1,0:T(4,12...) custom-call(f32[3,2048]{1,0:T(4,128)S(1)} %copy-done.4, bf16[64,2048]{1,0:T(8,128)(2,1)S(1)} %broadcast_select_fusion.h_ref, ...), custom_call_target="tpu_custom_call" | custom-call | tf_op jit(solution)/shard_map/pallas_call | solution.py:300
  17.4 0.0 copy-start.8
  17.4 0.6 copy-done.8
  18.0 0.6 copy-done.7
  18.7 0.1 compare_reduce_fusion.2
  18.7 0.9 %negate_select_fusion = f32[3,4096]{1,0:T(4,128)S(1)} fusion(f32[3,4096]{1,0:T(4,128)} %bitcast.33, pred[4096]{0:T(1024)(128)(4,1)S(1)} %lt.57), kind=kLoop, calls=%fused_computation.17 | loop fusion | flops 24576 | bytes 102400 | tf_op jit(solution)/shard_map/jit(_where)/select_n | solution.py:314
  19.6 0.1 compare_reduce_fusion
  19.8 0.3 fusion.1
  20.1 0.4 copy-done.18
  20.5 0.0 copy-done.19
  20.5 0.3 add_divide_fusion
  20.8 0.1 fusion.19
  20.9 0.1 pad_maximum_fusion.5
  20.9 0.1 reshape.65
  21.0 0.1 slice_reduce_fusion
  21.1 0.1 slice.33
  21.2 0.1 pad_maximum_fusion.4
  21.3 0.1 reshape.64
  21.4 0.1 fusion.18
  21.4 0.1 concatenate.36
  21.5 0.1 dynamic_slice.18
  21.6 0.1 broadcast_in_dim.38
  21.7 0.1 broadcast_in_dim.41
  21.8 0.1 broadcast_in_dim.40
  21.8 0.1 pad_maximum_fusion.1.q_ref
  22.0 0.1 broadcast_in_dim.39
  22.1 0.1 pad_maximum_fusion.p_ref
  22.2 0.8 %copy-done.9 = f32[48,3,128]{2,1,0:T(4,128)S(1)} copy-done((f32[48,3,128]{2,1,0:T(4,128)S(1)}, f32[48,3,128]{2,1,0:T(4,128)}, u32[]{:S(2)}) %copy-start.9) | copy-done | bytes 73752
  23.0 30.3 %shard_map.101 = (bf16[16,128,128]{2,1,0:T(8,128)(2,1)S(1)}, bf16[8,64,128]{2,1,0:T(8,128)(2,1)S(1)}) custom-call(s32[28,8]{1,0:T(8,128)S(1)} %copy-done.11, f32[28,8]{1,0:T(8,128)S(1)} %copy-done.10, bf16[16,128,128]{2,1,0:T(8,128)(2,1)S(1)} %bitcast.29, f32[128,128]{1,0:T(8,128)S(1)} %pad_maximum_fusion.p_ref, f32[128,128]{1,0:T(8,128)S(1)} %pad_maximum_fusion.1.q_ref, ...), custom_call_target="tpu_custom_call" | custom-call | tf_op jit(solution)/shard_map/pallas_call | solution.py:300
  53.2 0.0 copy-done.2
  53.3 0.0 copy-done.12
  53.3 12.4 %shard_map.102 = bf16[64,2048]{1,0:T(8,128)(2,1)S(1)} custom-call(s32[1]{0:T(128)S(6)} %copy.33.count_ref, bf16[64,2048]{1,0:T(8,128)(2,1)S(1)} %get-tuple-element.13.ta_ref, f32[64,2048]{1,0:T(8,128)S(1)} %get-tuple-element.14.tb_ref, bf16[2048,128]{1,0:T(8,128)(2,1)S(1)} %bitcast.30, bf16[64,2048]{1,0:T(8,128)(2,1)S(1)} %copy-done.1, ...), custom_call_target="tpu_custom_call" | custom-call | tf_op jit(solution)/shard_map/pallas_call | solution.py:300
  65.7 0.7 %copy.34 = bf16[64,2048]{1,0:T(8,128)(2,1)} copy(bf16[64,2048]{1,0:T(8,128)(2,1)S(1)} %shard_map.102) | data formatting | bytes 524288
  (26 shorter events, 0.2 us)
Async XLA Ops:
  0.0 5.1 %copy-start = (bf16[1,64,64]{2,1,0:T(8,128)(2,1)S(1)}, bf16[1,64,64]{2,1,0:T(8,128)(2,1)}, u32[]{:S(2)}) copy-start(bf16[1,64,64]{2,1,0:T(8,128)(2,1)} %param.16) | copy-start | bytes 24580
  0.0 1.8 %copy-start.17 = (s32[27,16]{0,1:T(8,128)S(1)}, s32[27,16]{0,1:T(8,128)}, u32[]{:S(2)}) copy-start(s32[27,16]{0,1:T(8,128)} %param.13) | copy-start | bytes 5188
  2.0 0.7 %copy-start.16 = (s32[27,16]{0,1:T(8,128)S(1)}, s32[27,16]{0,1:T(8,128)}, u32[]{:S(2)}) copy-start(s32[27,16]{0,1:T(8,128)} %param.12) | copy-start | bytes 5188
  2.8 0.8 %copy-start.15 = (s32[3,2048]{1,0:T(4,128)S(1)}, s32[3,2048]{1,0:T(4,128)}, u32[]{:S(2)}) copy-start(s32[3,2048]{1,0:T(4,128)} %param.15) | copy-start | bytes 73732
  2.8 1.4 %copy-start.13 = (bf16[1,128,192]{1,2,0:T(8,128)(2,1)S(1)}, bf16[1,128,192]{1,2,0:T(8,128)(2,1)}, u32[]{:S(2)}) copy-start(bf16[1,128,192]{1,2,0:T(8,128)(2,1)} %param.18) | copy-start | bytes 147460
  2.8 2.1 %copy-start.14 = (f32[1,64,64]{2,1,0:T(8,128)S(1)}, f32[1,64,64]{2,1,0:T(8,128)}, u32[]{:S(2)}) copy-start(f32[1,64,64]{2,1,0:T(8,128)} %param.17) | copy-start | bytes 49156
  2.9 2.1 %copy-start.1 = (bf16[64,2048]{1,0:T(8,128)(2,1)S(1)}, bf16[64,2048]{1,0:T(8,128)(2,1)}, u32[]{:S(2)}) copy-start(bf16[64,2048]{1,0:T(8,128)(2,1)} %h_ref.1) | copy-start | bytes 786436
  5.3 0.8 %copy-start.3 = (f32[3,2048]{1,0:T(4,128)S(1)}, f32[3,2048]{1,0:T(4,128)}, u32[]{:S(2)}) copy-start(f32[3,2048]{1,0:T(4,128)} %coords_ref.1) | copy-start | bytes 73732
  7.4 0.8 %copy-start.4 = (f32[3,2048]{1,0:T(4,128)S(1)}, f32[3,2048]{1,0:T(4,128)}, u32[]{:S(2)}) copy-start(f32[3,2048]{1,0:T(4,128)} %coords_ref.1) | copy-start | bytes 73732
  7.4 0.8 %copy-start.5 = (f32[16,3,128]{2,1,0:T(4,128)S(1)}, f32[16,3,128]{2,1,0:T(4,128)}, u32[]{:S(2)}) copy-start(f32[16,3,128]{2,1,0:T(4,128)} %copy.21.pos_ref) | copy-start | bytes 73732
  7.4 0.8 %copy-start.6 = (f32[3,2048]{1,0:T(4,128)S(1)}, f32[3,2048]{1,0:T(4,128)}, u32[]{:S(2)}) copy-start(f32[3,2048]{1,0:T(4,128)} %convert_element_type.20.k_ref) | copy-start | bytes 73732
  17.4 0.6 copy-start.8
  18.0 0.6 copy-start.7
  19.8 0.7 %copy-start.18 = (f32[31]{0:T(128)S(1)}, f32[31]{0:T(128)}, u32[]{:S(2)}) copy-start(f32[31]{0:T(128)} %multiply_add_fusion) | copy-start | bytes 376
  19.8 0.7 %copy-start.19 = (f32[33]{0:T(128)S(1)}, f32[33]{0:T(128)}, u32[]{:S(2)}) copy-start(f32[33]{0:T(128)} %multiply_add_fusion.1) | copy-start | bytes 400
  22.0 0.9 %copy-start.9 = (f32[48,3,128]{2,1,0:T(4,128)S(1)}, f32[48,3,128]{2,1,0:T(4,128)}, u32[]{:S(2)}) copy-start(f32[48,3,128]{2,1,0:T(4,128)} %copy-done.8) | copy-start | bytes 221188
  22.0 0.9 %copy-start.10 = (f32[28,8]{1,0:T(8,128)S(1)}, f32[28,8]{1,0:T(8,128)}, u32[]{:S(2)}) copy-start(f32[28,8]{1,0:T(8,128)} %pad_convert_fusion.live_ref) | copy-start | bytes 2692
  22.1 0.9 %copy-start.11 = (s32[28,8]{1,0:T(8,128)S(1)}, s32[28,8]{1,0:T(8,128)}, u32[]{:S(2)}) copy-start(s32[28,8]{1,0:T(8,128)} %pad.18.idx_ref) | copy-start | bytes 2692
  22.9 30.3 %copy-start.2 = (bf16[1,128,192]{2,1,0:T(8,128)(2,1)S(1)}, bf16[1,128,192]{2,1,0:T(8,128)(2,1)}, u32[]{:S(2)}) copy-start(bf16[1,128,192]{2,1,0:T(8,128)(2,1)} %copy.27) | copy-start | bytes 147460
  22.9 30.3 %copy-start.12 = (bf16[1,64,128]{2,1,0:T(8,128)(2,1)S(1)}, bf16[1,64,128]{2,1,0:T(8,128)(2,1)}, u32[]{:S(2)}) copy-start(bf16[1,64,128]{2,1,0:T(8,128)(2,1)} %param.19) | copy-start | bytes 49156
